TPU v7x, 512 devices: a whole 4x4x16 slice. The times are simulated.
512 devices in a mesh: dp: 4 (over x), expert: 128 (over z, y, core).
Axes of the slice: x: 4, y: 4, z: 16, core: 2. Of those that a mesh axis runs over, the one named last changes fastest.
Arguments:
- tokens: bfloat16 [8192, 2048], P(('dp', 'expert')), may hold values from -6 to 6
- cotangent: bfloat16 [8192, 2048], P(('dp', 'expert')), may hold values from -6 to 6
- expert_ids: int32 [8192, 8], P(('dp', 'expert')), may hold values from 0 to 127, all different within a row; in each aligned block of 16 rows (0 to 15, 16 to 31, ...) at most 2 rows name the same one
- gate_values: float32 [8192, 8], P(('dp', 'expert')), may hold values from 0.05 to 0.5
- gate_weight: bfloat16 [128, 2048, 384], P('expert', 'dp'), may hold values from -0.125 to 0.125
- up_weight: bfloat16 [128, 2048, 384], P('expert', 'dp'), may hold values from -0.125 to 0.125
- down_weight: bfloat16 [128, 2048, 384], P('expert', 'dp'), may hold values from -0.3125 to 0.3125
Outputs:
- mixed: bfloat16 [8192, 2048], P(('dp', 'expert'))
- input_grad: bfloat16 [8192, 2048], P(('dp', 'expert'))
- gate_grad: float32 [8192, 8], P(('dp', 'expert'))
- gate_weight_grad: float32 [128, 2048, 384], P('expert', 'dp')
- up_weight_grad: float32 [128, 2048, 384], P('expert', 'dp')
Inputs may be any that keep to these rules, and one draw needn't show every extreme that they name: `expert_ids`: each row names 8 different experts. Among the 16 rows of one device no expert is named more than 2 times.
All inputs are finite; a program needn't handle non-finite values.
Results may differ from a plain program's by a relative error of at most 0.012.
Values may be sent and summed in bfloat16 or wider, within the bound.
A program may use at most 64 MiB of HBM per device.

v0:
```python
import jax
import jax.numpy as jnp
from jax import lax
from jax.sharding import PartitionSpec as P


def body(tokens, cotangent, expert_ids, gate_values, gate_weight, up_weight, down_weight):
    tok_rows = tokens.shape[0]
    feature_width = tokens.shape[1]
    top_count = expert_ids.shape[1]
    experts = lax.axis_size("expert")
    routed = tok_rows * top_count
    capacity = min(tok_rows, max(2, (routed + experts - 1) // experts + 1))
    flat_ids = expert_ids.reshape(routed)
    onehot = (flat_ids[:, None] == jnp.arange(experts, dtype=jnp.int32)[None, :]).astype(jnp.int32)
    earlier = jnp.cumsum(onehot, axis=0) - onehot
    slot_rank = jnp.sum(earlier * onehot, axis=1)
    target = flat_ids * capacity + slot_rank
    owner_row = jnp.arange(routed, dtype=jnp.int32) // top_count
    gate_flat = gate_values.reshape(routed)
    picked = tokens[owner_row]
    scaled = (gate_flat[:, None] * cotangent[owner_row].astype(jnp.float32)).astype(jnp.bfloat16)
    slot_count = experts * capacity
    send_rows = jnp.zeros((slot_count, feature_width), jnp.bfloat16).at[target].set(picked)
    send_rows = send_rows.reshape(experts, capacity, feature_width)
    send_grads = jnp.zeros((slot_count, feature_width), jnp.bfloat16).at[target].set(scaled)
    send_grads = send_grads.reshape(experts, capacity, feature_width)
    gate_full, up_full, down_full = (
        lax.all_gather(gate_weight, "dp", axis=1, tiled=True),
        lax.all_gather(up_weight, "dp", axis=1, tiled=True),
        lax.all_gather(down_weight, "dp", axis=1, tiled=True),
    )
    gate_mat = gate_full[0]
    up_mat = up_full[0]
    arrived = lax.all_to_all(send_rows, "expert", split_axis=0, concat_axis=0, tiled=True)
    rows = arrived.reshape(slot_count, feature_width)
    hidden_gate = jnp.dot(rows, gate_mat, preferred_element_type=jnp.float32)
    hidden_up = jnp.dot(rows, up_mat, preferred_element_type=jnp.float32)
    down_mat = down_full[0]
    sigma = jax.nn.sigmoid(hidden_gate)
    active = (hidden_gate * sigma * hidden_up).astype(jnp.bfloat16)
    contract_last = (((1,), (1,)), ((), ()))
    outputs = lax.dot_general(
        active, down_mat, contract_last, preferred_element_type=jnp.float32
    ).astype(jnp.bfloat16)
    outputs = outputs.reshape(experts, capacity, feature_width)
    returned = lax.all_to_all(outputs, "expert", split_axis=0, concat_axis=0, tiled=True)
    arrived_grads = lax.all_to_all(send_grads, "expert", split_axis=0, concat_axis=0, tiled=True)
    grad_rows = arrived_grads.reshape(slot_count, feature_width)
    grad_active = jnp.dot(grad_rows, down_mat, preferred_element_type=jnp.float32)
    grad_up = (grad_active * hidden_gate * sigma).astype(jnp.bfloat16)
    grad_gate = (grad_active * hidden_up * sigma * (1.0 + hidden_gate * (1.0 - sigma))).astype(
        jnp.bfloat16
    )
    input_rows = lax.dot_general(
        grad_gate, gate_mat, contract_last, preferred_element_type=jnp.float32
    )
    input_rows = input_rows + lax.dot_general(
        grad_up, up_mat, contract_last, preferred_element_type=jnp.float32
    )
    input_rows = input_rows.astype(jnp.bfloat16).reshape(experts, capacity, feature_width)
    returned_grads = lax.all_to_all(input_rows, "expert", split_axis=0, concat_axis=0, tiled=True)
    contract_rows = (((0,), (0,)), ((), ()))
    gate_part = lax.dot_general(rows, grad_gate, contract_rows, preferred_element_type=jnp.float32)
    up_part = lax.dot_general(rows, grad_up, contract_rows, preferred_element_type=jnp.float32)
    gate_weight_grad, up_weight_grad = (
        lax.psum_scatter(
            gate_part[None].astype(jnp.bfloat16), "dp", scatter_dimension=1, tiled=True
        ).astype(jnp.float32),
        lax.psum_scatter(
            up_part[None].astype(jnp.bfloat16), "dp", scatter_dimension=1, tiled=True
        ).astype(jnp.float32),
    )
    back_rows = returned.reshape(slot_count, feature_width)[target].astype(jnp.float32)
    back_rows = back_rows.reshape(tok_rows, top_count, feature_width)
    back_grads = returned_grads.reshape(slot_count, feature_width)[target].astype(jnp.float32)
    back_grads = back_grads.reshape(tok_rows, top_count, feature_width)
    weights_here = gate_flat.reshape(tok_rows, top_count)
    mixed = jnp.sum(weights_here[:, :, None] * back_rows, axis=1).astype(jnp.bfloat16)
    gate_grad = jnp.sum(back_rows * cotangent.astype(jnp.float32)[:, None, :], axis=2)
    input_grad = jnp.sum(back_grads, axis=1).astype(jnp.bfloat16)
    return (mixed, input_grad, gate_grad, gate_weight_grad, up_weight_grad)


def solution(mesh):
    placed = (
        P(("dp", "expert"), None),
        P(("dp", "expert"), None),
        P(("dp", "expert"), None),
        P(("dp", "expert"), None),
        P("expert", "dp", None),
        P("expert", "dp", None),
        P("expert", "dp", None),
    )
    return jax.shard_map(
        body,
        mesh=mesh,
        in_specs=placed,
        out_specs=(
            P(("dp", "expert"), None),
            P(("dp", "expert"), None),
            P(("dp", "expert"), None),
            P("expert", "dp", None),
            P("expert", "dp", None),
        ),
        check_vma=False,
    )
```

profile of v0, /device:TPU:33, one launch (start us, length us, event | category | flops | bytes accessed | tf_op | source)
XLA Modules:
  0.0 292.1 jit_solution(706173469473217055)
XLA Ops:
  9.4 3.4 %scatter_custom_fusion = bf16[256,2048]{1,0:T(8,128)(2,1)S(1)} fusion(s32[128]{0:T(128)S(1)} %fusion.24, bf16[16,2048]{1,0:T(8,128)(2,1)S(1)} %copy-done, s32[1024]{0:T(1024)S(1)} %pad_clamp_fusion.1, bf16[]{:T(256)} %constant.26.clone.1), kind=kCustom, calls=%fused_computation.30 | custom fusion | bytes 1048578 | tf_op jit(solution)/shard_map/scatter | solution.py:24
  14.3 19.6 %all-to-all-start = ((bf16[128,2,2048]{2,1,0:T(2,128)(2,1)}), bf16[128,2,2048]{2,1,0:T(2,128)(2,1)S(1)}, u32[]{:S(2)}, u32[]{:S(2)}) async-start(bf16[128,2,2048]{2,1,0:T(2,128)(2,1)} %reshape.128), calls=%async_computation | async-start | bytes 2097152 | tf_op jit(solution)/shard_map/all_to_all | solution.py:35
  35.6 3.4 %scatter_custom_fusion.1 = bf16[256,2048]{1,0:T(8,128)(2,1)S(1)} fusion(s32[128]{0:T(128)S(1)} %fusion.24, f32[128]{0:T(128)S(1)} %mul.81, bf16[]{:T(256)} %constant.26.clone.1, bf16[16,2048]{1,0:T(8,128)(2,1)S(1)} %copy-done.3, s32[1024]{0:T(1024)S(1)} %pad_clamp_fusion.1), kind=kCustom, calls=%fused_computation.28 | custom fusion | flops 786432 | bytes 1118722 | tf_op jit(solution)/shard_map/scatter | solution.py:26
  39.0 1.5 reshape.132
  40.5 49.0 %all-to-all-done = bf16[128,2,2048]{2,1,0:T(2,128)(2,1)S(1)} async-done(((bf16[128,2,2048]{2,1,0:T(2,128)(2,1)}), bf16[128,2,2048]{2,1,0:T(2,128)(2,1)S(1)}, u32[]{:S(2)}, u32[]{:S(2)}) %all-to-all-start) | async-done | bytes 1048608 | tf_op jit(solution)/shard_map/all_to_all | solution.py:35
  89.5 6.4 %all-to-all-start.2 = ((bf16[128,2,2048]{2,1,0:T(2,128)(2,1)}), bf16[128,2,2048]{2,1,0:T(2,128)(2,1)S(1)}, u32[]{:S(2)}, u32[]{:S(2)}) async-start(bf16[128,2,2048]{2,1,0:T(2,128)(2,1)} %reshape.132), calls=%async_computation.2 | async-start | bytes 2097152 | tf_op jit(solution)/shard_map/all_to_all | solution.py:48
  97.2 2.9 fusion.7
  100.0 8.2 %all-gather.4.cloned.1.call-done = bf16[1,2048,384]{2,1,0:T(8,128)(2,1)} async-done(((bf16[1,512,384]{2,1,0:T(8,128)(2,1)}), bf16[1,2048,384]{2,1,0:T(8,128)(2,1)}) %all-gather.4.cloned.1.call-update) | async-done | bytes 1572880 | tf_op jit(solution)/shard_map/all_gather | solution.py:29
  108.2 2.9 fusion.11
  111.1 33.6 %all-gather.8.cloned.1.call-done = bf16[1,2048,384]{2,1,0:T(8,128)(2,1)} async-done(((bf16[1,512,384]{2,1,0:T(8,128)(2,1)}), bf16[1,2048,384]{2,1,0:T(8,128)(2,1)}) %all-gather.8.cloned.1.call-update) | async-done | bytes 1572880 | tf_op jit(solution)/shard_map/all_gather | solution.py:31
  144.7 2.4 convolution_convert_fusion.2
  147.1 1.5 reshape.130
  148.6 2.9 %all-to-all-done.2 = bf16[128,2,2048]{2,1,0:T(2,128)(2,1)S(1)} async-done(((bf16[128,2,2048]{2,1,0:T(2,128)(2,1)}), bf16[128,2,2048]{2,1,0:T(2,128)(2,1)S(1)}, u32[]{:S(2)}, u32[]{:S(2)}) %all-to-all-start.2) | async-done | bytes 1048608 | tf_op jit(solution)/shard_map/all_to_all | solution.py:48
  151.6 14.3 %all-to-all-start.1 = ((bf16[128,2,2048]{2,1,0:T(2,128)(2,1)}), bf16[128,2,2048]{2,1,0:T(2,128)(2,1)}, u32[]{:S(2)}, u32[]{:S(2)}) async-start(bf16[128,2,2048]{2,1,0:T(2,128)(2,1)} %reshape.130), calls=%async_computation.1 | async-start | bytes 2097152 | tf_op jit(solution)/shard_map/all_to_all | solution.py:47
  166.4 2.4 multiply_convert_fusion.2
  168.7 1.9 fusion
  174.4 46.8 %all-to-all-done.1 = bf16[128,2,2048]{2,1,0:T(2,128)(2,1)} async-done(((bf16[128,2,2048]{2,1,0:T(2,128)(2,1)}), bf16[128,2,2048]{2,1,0:T(2,128)(2,1)}, u32[]{:S(2)}, u32[]{:S(2)}) %all-to-all-start.1) | async-done | bytes 1048608 | tf_op jit(solution)/shard_map/all_to_all | solution.py:47
  221.1 6.4 %all-to-all-start.3 = ((bf16[128,2,2048]{2,1,0:T(2,128)(2,1)}), bf16[128,2,2048]{2,1,0:T(2,128)(2,1)S(1)}, u32[]{:S(2)}, u32[]{:S(2)}) async-start(bf16[128,2,2048]{2,1,0:T(2,128)(2,1)} %reshape.134), calls=%async_computation.3 | async-start | bytes 2097152 | tf_op jit(solution)/shard_map/all_to_all | solution.py:62
  227.8 1.9 fusion.1
  229.8 1.9 convert_element_type.76
  231.8 31.1 %reduce-scatter.5.cloned.1.call-done = bf16[1,512,384]{2,1,0:T(8,128)(2,1)} async-done(((bf16[1,2048,384]{2,1,0:T(8,128)(2,1)}), bf16[1,512,384]{2,1,0:T(8,128)(2,1)}) %reduce-scatter.5.cloned.1.call-update) | async-done | bytes 393232 | tf_op jit(solution)/shard_map/reduce_scatter | solution.py:70
  262.8 1.9 convert_element_type.79
  267.2 1.7 fusion.14
  269.5 13.7 %all-to-all-done.3 = bf16[128,2,2048]{2,1,0:T(2,128)(2,1)S(1)} async-done(((bf16[128,2,2048]{2,1,0:T(2,128)(2,1)}), bf16[128,2,2048]{2,1,0:T(2,128)(2,1)S(1)}, u32[]{:S(2)}, u32[]{:S(2)}) %all-to-all-start.3) | async-done | bytes 1048608 | tf_op jit(solution)/shard_map/all_to_all | solution.py:62
  (49 shorter events, 16.4 us)
Async XLA Ops:
  7.2 2.2 copy-start
  14.3 21.1 %copy-start.4 = (f32[16,8]{0,1:T(8,128)S(1)}, f32[16,8]{0,1:T(8,128)}, u32[]{:S(2)}) copy-start(f32[16,8]{0,1:T(8,128)} %param.10) | copy-start | bytes 1540
  14.3 21.3 %copy-start.3 = (bf16[16,2048]{1,0:T(8,128)(2,1)S(1)}, bf16[16,2048]{1,0:T(8,128)(2,1)}, u32[]{:S(2)}) copy-start(bf16[16,2048]{1,0:T(8,128)(2,1)} %param.8) | copy-start | bytes 196612
  14.3 75.2 %all-to-all-start = ((bf16[128,2,2048]{2,1,0:T(2,128)(2,1)}), bf16[128,2,2048]{2,1,0:T(2,128)(2,1)S(1)}, u32[]{:S(2)}, u32[]{:S(2)}) async-start(bf16[128,2,2048]{2,1,0:T(2,128)(2,1)} %reshape.128), calls=%async_computation | async-start | bytes 2097152 | tf_op jit(solution)/shard_map/all_to_all | solution.py:35
  33.9 63.3 %all-gather.6.cloned.1.call-start = ((), (), s32[]{:S(2)}) async-start(), calls=%async_computation.7 | async-start | bytes 1966080 | tf_op jit(solution)/shard_map/all_gather | solution.py:30
  34.6 73.6 %all-gather.4.cloned.1.call-start = ((), (), s32[]{:S(2)}) async-start(), calls=%async_computation.6 | async-start | bytes 1966080 | tf_op jit(solution)/shard_map/all_gather | solution.py:29
  89.5 62.1 %all-to-all-start.2 = ((bf16[128,2,2048]{2,1,0:T(2,128)(2,1)}), bf16[128,2,2048]{2,1,0:T(2,128)(2,1)S(1)}, u32[]{:S(2)}, u32[]{:S(2)}) async-start(bf16[128,2,2048]{2,1,0:T(2,128)(2,1)} %reshape.132), calls=%async_computation.2 | async-start | bytes 2097152 | tf_op jit(solution)/shard_map/all_to_all | solution.py:48
  96.0 48.7 %all-gather.8.cloned.1.call-start = ((), (), s32[]{:S(2)}) async-start(), calls=%async_computation.8 | async-start | bytes 1966080 | tf_op jit(solution)/shard_map/all_gather | solution.py:31
  151.6 69.6 %all-to-all-start.1 = ((bf16[128,2,2048]{2,1,0:T(2,128)(2,1)}), bf16[128,2,2048]{2,1,0:T(2,128)(2,1)}, u32[]{:S(2)}, u32[]{:S(2)}) async-start(bf16[128,2,2048]{2,1,0:T(2,128)(2,1)} %reshape.130), calls=%async_computation.1 | async-start | bytes 2097152 | tf_op jit(solution)/shard_map/all_to_all | solution.py:47
  165.9 64.0 %reduce-scatter.3.cloned.1.call-start = ((), (), s32[]{:S(2)}) async-start(), calls=%async_computation.9 | async-start | bytes 1966080 | tf_op jit(solution)/shard_map/reduce_scatter | solution.py:67
  168.7 1.9 copy-start.2
  170.7 1.4 copy-start.1
  221.1 62.1 %all-to-all-start.3 = ((bf16[128,2,2048]{2,1,0:T(2,128)(2,1)}), bf16[128,2,2048]{2,1,0:T(2,128)(2,1)S(1)}, u32[]{:S(2)}, u32[]{:S(2)}) async-start(bf16[128,2,2048]{2,1,0:T(2,128)(2,1)} %reshape.134), calls=%async_computation.3 | async-start | bytes 2097152 | tf_op jit(solution)/shard_map/all_to_all | solution.py:62
  227.6 35.3 %reduce-scatter.5.cloned.1.call-start = ((), (), s32[]{:S(2)}) async-start(), calls=%async_computation.10 | async-start | bytes 1966080 | tf_op jit(solution)/shard_map/reduce_scatter | solution.py:70
Sparse Core Ops, SparseCore 0:
  36.8 34.8 all-gather.5
  73.9 34.3 all-gather.3
  110.3 34.3 all-gather.7
  170.8 31.8 reduce-scatter.2
  230.9 31.8 reduce-scatter.4
where the time goes:
time: 293 us; the launch traced here: 292 us
  waiting for transfers between devices  187 us (64%)
  starting transfers between devices  47.4 us (16%)
  local copies, waits for them, and re-layouts  16.5 us (6%)
  matrix products  15.8 us (5%)
  between operations  14 us (5%)
  other arithmetic  11.1 us (4%)
    all_to_all x1, waiting for transfers between devices, body(): lax.all_to_all(send_rows, 'expert', split_axis=0, concat_axis=0, tiled=True)  49 us
    all_to_all x1, waiting for transfers between devices, body(): lax.all_to_all(outputs, 'expert', split_axis=0, concat_axis=0, tiled=True)  46.8 us
    all_gather x1, waiting for transfers between devices, body(): lax.all_gather(down_weight, 'dp', axis=1, tiled=True)  33.6 us
    reduce_scatter x1, waiting for transfers between devices, body(): lax.psum_scatter(up_part[None].astype(jnp.bfloat16), 'dp', scatter_dimens...  31.1 us
    all_to_all x1, starting transfers between devices, body(): lax.all_to_all(send_rows, 'expert', split_axis=0, concat_axis=0, tiled=True)  19.6 us
    all_to_all x1, starting transfers between devices, body(): lax.all_to_all(outputs, 'expert', split_axis=0, concat_axis=0, tiled=True)  14.3 us
    all_to_all x1, waiting for transfers between devices, body(): lax.all_to_all(input_rows, 'expert', split_axis=0, concat_axis=0, tiled=T...  13.7 us
    all_gather x1, waiting for transfers between devices, body(): lax.all_gather(gate_weight, 'dp', axis=1, tiled=True)  8.2 us
  transfers between devices with their start and end apart: 9, of which 7 were waited for; matrix products, arithmetic and copies ran while one was open for 11% of the time, Pallas kernels for 0%

commit v1 on v0

--- a/solution.py
+++ b/solution.py
@@ -2,6 +2,14 @@
 import jax.numpy as jnp
 from jax import lax
 from jax.sharding import PartitionSpec as P
+
+
+def gather_by_exchange(array, axis, dim):
+    size = lax.axis_size(axis)
+    repeats = [size if d == dim else 1 for d in range(array.ndim)]
+    return lax.all_to_all(
+        jnp.tile(array, repeats), axis, split_axis=dim, concat_axis=dim, tiled=True
+    )
 
 
 def body(tokens, cotangent, expert_ids, gate_values, gate_weight, up_weight, down_weight):
@@ -26,7 +34,7 @@
     send_grads = jnp.zeros((slot_count, feature_width), jnp.bfloat16).at[target].set(scaled)
     send_grads = send_grads.reshape(experts, capacity, feature_width)
     gate_full, up_full, down_full = (
-        lax.all_gather(gate_weight, "dp", axis=1, tiled=True),
+        gather_by_exchange(gate_weight, "dp", 1),
         lax.all_gather(up_weight, "dp", axis=1, tiled=True),
         lax.all_gather(down_weight, "dp", axis=1, tiled=True),
     )

time: 293 us -> 376 us (1.28)
  local copies, waits for them, and re-layouts: 16.5 us -> 55.1 us
  other arithmetic: 11.1 us -> 44.9 us
  waiting for transfers between devices: 187 us -> 197 us
    unnamed x0 -> x1, other arithmetic: none -> 34.4 us
    another operation x0 -> x2, local copies, waits for them, and re-layouts: none -> 31.3 us  [gather_by_exchange(): jnp.tile(array, repeats)]
    all_to_all x0 -> x1, waiting for transfers between devices: none -> 14.1 us  [gather_by_exchange(): lax.all_to_all(jnp.tile(array, repeats), axis, split_axis=dim, concat_axi...]
    all_to_all x1, waiting for transfers between devices: 2.94 us -> 15.7 us  [body(): lax.all_to_all(send_grads, 'expert', split_axis=0, concat_axis=0, tiled=T...]
    all_gather x1, waiting for transfers between devices: 33.6 us -> 24.8 us  [body(): lax.all_gather(down_weight, 'dp', axis=1, tiled=True)]
    all_gather x1 -> x0, waiting for transfers between devices: 8.2 us -> none  [body(): lax.all_gather(gate_weight, 'dp', axis=1, tiled=True)]
    all_to_all x1, starting transfers between devices: 14.3 us -> 6.44 us  [body(): lax.all_to_all(outputs, 'expert', split_axis=0, concat_axis=0, tiled=True)]
    unnamed x13 -> x18, local copies, waits for them, and re-layouts: 2.17 us -> 7.93 us
  transfers between devices with their start and end apart: 9 -> 9, of which waited for: 7 -> 7; matrix products, arithmetic and copies ran while one was open for 11% -> 12% of each run, Pallas kernels for 0% -> 0%
where the time goes in v1:
time: 376 us; the launch traced here: 375 us
  waiting for transfers between devices  197 us (52%)
  local copies, waits for them, and re-layouts  55.1 us (15%)
  starting transfers between devices  45 us (12%)
  other arithmetic  44.9 us (12%)
  matrix products  18.6 us (5%)
  between operations  14 us (4%)
    all_to_all x1, waiting for transfers between devices, body(): lax.all_to_all(send_rows, 'expert', split_axis=0, concat_axis=0, tiled=True)  49.4 us
    all_to_all x1, waiting for transfers between devices, body(): lax.all_to_all(outputs, 'expert', split_axis=0, concat_axis=0, tiled=True)  44.4 us
    unnamed x1, other arithmetic  34.4 us
    another operation x2, local copies, waits for them, and re-layouts, gather_by_exchange(): jnp.tile(array, repeats)  31.3 us
    reduce_scatter x1, waiting for transfers between devices, body(): lax.psum_scatter(up_part[None].astype(jnp.bfloat16), 'dp', scatter_dimens...  30.6 us
    all_gather x1, waiting for transfers between devices, body(): lax.all_gather(down_weight, 'dp', axis=1, tiled=True)  24.8 us
    all_to_all x1, starting transfers between devices, body(): lax.all_to_all(send_rows, 'expert', split_axis=0, concat_axis=0, tiled=True)  21.1 us
    all_to_all x1, waiting for transfers between devices, body(): lax.all_to_all(input_rows, 'expert', split_axis=0, concat_axis=0, tiled=T...  17 us
  transfers between devices with their start and end apart: 9, of which 7 were waited for; matrix products, arithmetic and copies ran while one was open for 12% of the time, Pallas kernels for 0%

profile of v1, /device:TPU:33, one launch (start us, length us, event | category | flops | bytes accessed | tf_op | source)
XLA Modules:
  0.0 374.9 jit_solution(13183726693425576984)
XLA Ops:
  8.3 30.1 %copy.41 = bf16[1,2048,384]{2,0,1:T(2,128)(2,1)S(1)} copy(bf16[1,2048,384]{2,1,0:T(8,128)(2,1)S(1)} %bitcast.53) | data formatting | bytes 3145728 | tf_op jit(solution)/shard_map/tile | solution.py:11
  39.0 34.4 %reduce.5 = bf16[2048,384]{1,0:T(8,128)(2,1)} reduce(bf16[2048,1,384]{2,1,0:T(2,128)(2,1)S(1)} %bitcast.50, bf16[]{:T(256)} %broadcast.139), dimensions={1}, to_apply=%bitcast.49.reduce_sub_computation | reduce | bytes 3145730
  73.4 3.8 %reshape.207 = bf16[4,2,98304]{2,1,0:T(2,128)(2,1)} reshape(bf16[2048,384]{1,0:T(8,128)(2,1)} %reduce.5) | data formatting | bytes 3145728
  77.2 4.1 %all-to-all-start.1 = ((bf16[4,2,98304]{2,1,0:T(2,128)(2,1)}), bf16[4,2,98304]{2,1,0:T(2,128)(2,1)S(1)}, u32[]{:S(2)}, u32[]{:S(2)}) async-start(bf16[4,2,98304]{2,1,0:T(2,128)(2,1)} %reshape.207), calls=%async_computation.1 | async-start | bytes 3145728 | tf_op jit(solution)/shard_map/all_to_all | solution.py:10
  82.1 3.4 scatter_custom_fusion
  87.0 14.1 %all-to-all-done.1 = bf16[4,2,98304]{2,1,0:T(2,128)(2,1)S(1)} async-done(((bf16[4,2,98304]{2,1,0:T(2,128)(2,1)}), bf16[4,2,98304]{2,1,0:T(2,128)(2,1)S(1)}, u32[]{:S(2)}, u32[]{:S(2)}) %all-to-all-start.1) | async-done | bytes 1572896 | tf_op jit(solution)/shard_map/all_to_all | solution.py:10
  101.1 21.1 %all-to-all-start = ((bf16[128,2,2048]{2,1,0:T(2,128)(2,1)}), bf16[128,2,2048]{2,1,0:T(2,128)(2,1)}, u32[]{:S(2)}, u32[]{:S(2)}) async-start(bf16[128,2,2048]{2,1,0:T(2,128)(2,1)} %reshape.134), calls=%async_computation | async-start | bytes 2097152 | tf_op jit(solution)/shard_map/all_to_all | solution.py:43
  123.2 3.4 scatter_custom_fusion.1
  128.1 49.4 %all-to-all-done = bf16[128,2,2048]{2,1,0:T(2,128)(2,1)} async-done(((bf16[128,2,2048]{2,1,0:T(2,128)(2,1)}), bf16[128,2,2048]{2,1,0:T(2,128)(2,1)}, u32[]{:S(2)}, u32[]{:S(2)}) %all-to-all-start) | async-done | bytes 1048608 | tf_op jit(solution)/shard_map/all_to_all | solution.py:43
  177.5 6.4 %all-to-all-start.3 = ((bf16[128,2,2048]{2,1,0:T(2,128)(2,1)}), bf16[128,2,2048]{2,1,0:T(2,128)(2,1)S(1)}, u32[]{:S(2)}, u32[]{:S(2)}) async-start(bf16[128,2,2048]{2,1,0:T(2,128)(2,1)} %reshape.138), calls=%async_computation.3 | async-start | bytes 2097152 | tf_op jit(solution)/shard_map/all_to_all | solution.py:56
  184.7 2.8 reshape.208
  189.0 3.3 fusion.5
  192.4 2.9 fusion.11
  195.2 24.8 %all-gather.5.cloned.1.call-done = bf16[1,2048,384]{2,1,0:T(8,128)(2,1)} async-done(((bf16[1,512,384]{2,1,0:T(8,128)(2,1)}), bf16[1,2048,384]{2,1,0:T(8,128)(2,1)}) %all-gather.5.cloned.1.call-update) | async-done | bytes 1572880 | tf_op jit(solution)/shard_map/all_gather | solution.py:39
  220.0 2.4 convolution_convert_fusion.2
  223.9 15.7 %all-to-all-done.3 = bf16[128,2,2048]{2,1,0:T(2,128)(2,1)S(1)} async-done(((bf16[128,2,2048]{2,1,0:T(2,128)(2,1)}), bf16[128,2,2048]{2,1,0:T(2,128)(2,1)S(1)}, u32[]{:S(2)}, u32[]{:S(2)}) %all-to-all-start.3) | async-done | bytes 1048608 | tf_op jit(solution)/shard_map/all_to_all | solution.py:56
  239.6 6.4 %all-to-all-start.2 = ((bf16[128,2,2048]{2,1,0:T(2,128)(2,1)}), bf16[128,2,2048]{2,1,0:T(2,128)(2,1)S(1)}, u32[]{:S(2)}, u32[]{:S(2)}) async-start(bf16[128,2,2048]{2,1,0:T(2,128)(2,1)} %reshape.136), calls=%async_computation.2 | async-start | bytes 2097152 | tf_op jit(solution)/shard_map/all_to_all | solution.py:55
  247.5 2.7 multiply_convert_fusion.2
  252.2 2.7 fusion.3
  257.2 44.4 %all-to-all-done.2 = bf16[128,2,2048]{2,1,0:T(2,128)(2,1)S(1)} async-done(((bf16[128,2,2048]{2,1,0:T(2,128)(2,1)}), bf16[128,2,2048]{2,1,0:T(2,128)(2,1)S(1)}, u32[]{:S(2)}, u32[]{:S(2)}) %all-to-all-start.2) | async-done | bytes 1048608 | tf_op jit(solution)/shard_map/all_to_all | solution.py:55
  301.6 6.4 %all-to-all-start.4 = ((bf16[128,2,2048]{2,1,0:T(2,128)(2,1)}), bf16[128,2,2048]{2,1,0:T(2,128)(2,1)S(1)}, u32[]{:S(2)}, u32[]{:S(2)}) async-start(bf16[128,2,2048]{2,1,0:T(2,128)(2,1)} %reshape.140), calls=%async_computation.4 | async-start | bytes 2097152 | tf_op jit(solution)/shard_map/all_to_all | solution.py:70
  310.1 1.9 convert_element_type.76
  312.1 30.6 %reduce-scatter.5.cloned.1.call-done = bf16[1,512,384]{2,1,0:T(8,128)(2,1)} async-done(((bf16[1,2048,384]{2,1,0:T(8,128)(2,1)}), bf16[1,512,384]{2,1,0:T(8,128)(2,1)}) %reduce-scatter.5.cloned.1.call-update) | async-done | bytes 393232 | tf_op jit(solution)/shard_map/reduce_scatter | solution.py:78
  346.7 17.0 %all-to-all-done.4 = bf16[128,2,2048]{2,1,0:T(2,128)(2,1)S(1)} async-done(((bf16[128,2,2048]{2,1,0:T(2,128)(2,1)}), bf16[128,2,2048]{2,1,0:T(2,128)(2,1)S(1)}, u32[]{:S(2)}, u32[]{:S(2)}) %all-to-all-start.4) | async-done | bytes 1048608 | tf_op jit(solution)/shard_map/all_to_all | solution.py:70
  (56 shorter events, 26.6 us)
Async XLA Ops:
  7.2 74.9 %copy-start = (bf16[16,2048]{1,0:T(8,128)(2,1)S(1)}, bf16[16,2048]{1,0:T(8,128)(2,1)}, u32[]{:S(2)}) copy-start(bf16[16,2048]{1,0:T(8,128)(2,1)} %param.7) | copy-start | bytes 196612
  77.2 4.1 %copy-start.4 = (s32[16,8]{0,1:T(8,128)S(1)}, s32[16,8]{0,1:T(8,128)}, u32[]{:S(2)}) copy-start(s32[16,8]{0,1:T(8,128)} %param.9) | copy-start | bytes 1540
  77.2 23.9 %all-to-all-start.1 = ((bf16[4,2,98304]{2,1,0:T(2,128)(2,1)}), bf16[4,2,98304]{2,1,0:T(2,128)(2,1)S(1)}, u32[]{:S(2)}, u32[]{:S(2)}) async-start(bf16[4,2,98304]{2,1,0:T(2,128)(2,1)} %reshape.207), calls=%async_computation.1 | async-start | bytes 3145728 | tf_op jit(solution)/shard_map/all_to_all | solution.py:10
  87.0 36.0 %copy-start.5 = (f32[16,8]{0,1:T(8,128)S(1)}, f32[16,8]{0,1:T(8,128)}, u32[]{:S(2)}) copy-start(f32[16,8]{0,1:T(8,128)} %param.10) | copy-start | bytes 1540
  87.0 36.2 %copy-start.3 = (bf16[16,2048]{1,0:T(8,128)(2,1)S(1)}, bf16[16,2048]{1,0:T(8,128)(2,1)}, u32[]{:S(2)}) copy-start(bf16[16,2048]{1,0:T(8,128)(2,1)} %param.8) | copy-start | bytes 196612
  101.1 76.4 %all-to-all-start = ((bf16[128,2,2048]{2,1,0:T(2,128)(2,1)}), bf16[128,2,2048]{2,1,0:T(2,128)(2,1)}, u32[]{:S(2)}, u32[]{:S(2)}) async-start(bf16[128,2,2048]{2,1,0:T(2,128)(2,1)} %reshape.134), calls=%async_computation | async-start | bytes 2097152 | tf_op jit(solution)/shard_map/all_to_all | solution.py:43
  122.2 70.1 %all-gather.3.cloned.1.call-start = ((), (), s32[]{:S(2)}) async-start(), calls=%async_computation.7 | async-start | bytes 1966080 | tf_op jit(solution)/shard_map/all_gather | solution.py:38
  177.5 62.1 %all-to-all-start.3 = ((bf16[128,2,2048]{2,1,0:T(2,128)(2,1)}), bf16[128,2,2048]{2,1,0:T(2,128)(2,1)S(1)}, u32[]{:S(2)}, u32[]{:S(2)}) async-start(bf16[128,2,2048]{2,1,0:T(2,128)(2,1)} %reshape.138), calls=%async_computation.3 | async-start | bytes 2097152 | tf_op jit(solution)/shard_map/all_to_all | solution.py:56
  184.0 36.0 %all-gather.5.cloned.1.call-start = ((), (), s32[]{:S(2)}) async-start(), calls=%async_computation.8 | async-start | bytes 1966080 | tf_op jit(solution)/shard_map/all_gather | solution.py:39
  239.6 62.1 %all-to-all-start.2 = ((bf16[128,2,2048]{2,1,0:T(2,128)(2,1)}), bf16[128,2,2048]{2,1,0:T(2,128)(2,1)S(1)}, u32[]{:S(2)}, u32[]{:S(2)}) async-start(bf16[128,2,2048]{2,1,0:T(2,128)(2,1)} %reshape.136), calls=%async_computation.2 | async-start | bytes 2097152 | tf_op jit(solution)/shard_map/all_to_all | solution.py:55
  246.0 64.1 %reduce-scatter.3.cloned.1.call-start = ((), (), s32[]{:S(2)}) async-start(), calls=%async_computation.9 | async-start | bytes 1966080 | tf_op jit(solution)/shard_map/reduce_scatter | solution.py:75
  252.1 2.8 copy-start.1
  301.6 62.1 %all-to-all-start.4 = ((bf16[128,2,2048]{2,1,0:T(2,128)(2,1)}), bf16[128,2,2048]{2,1,0:T(2,128)(2,1)S(1)}, u32[]{:S(2)}, u32[]{:S(2)}) async-start(bf16[128,2,2048]{2,1,0:T(2,128)(2,1)} %reshape.140), calls=%async_computation.4 | async-start | bytes 2097152 | tf_op jit(solution)/shard_map/all_to_all | solution.py:70
  308.1 34.6 %reduce-scatter.5.cloned.1.call-start = ((), (), s32[]{:S(2)}) async-start(), calls=%async_computation.10 | async-start | bytes 1966080 | tf_op jit(solution)/shard_map/reduce_scatter | solution.py:78
  364.1 1.9 copy-start.2
Sparse Core Ops, SparseCore 0:
  125.2 33.0 all-gather.2
  186.9 33.0 all-gather.4
  252.3 31.1 reduce-scatter.2
  311.4 31.1 reduce-scatter.4
